TPU v7x, 256 devices: a whole 4x4x8 slice. The times are simulated.
256 devices in a mesh: wide: 16 (over x, z_lo), narrow: 16 (over z_hi, y, core).
Axes of the slice: x: 4, y: 4, z: 8 (z_hi: 2, z_lo: 4; z = z_hi * 4 + z_lo), core: 2. Of those that a mesh axis runs over, the one named last changes fastest.
Arguments:
- basis: float32 [65536, 8192], P('wide', 'narrow'), may hold values from -0.0234375 to 0.0234375
- conf_values: float32 [8192], P('narrow'), may hold values from 0.5 to 8
- task_basis: float32 [128, 128], replicated, may hold values from -0.5 to 0.5
- task_values: float32 [128], replicated, may hold values from 0.5 to 4
- noise: float32 [1], replicated, may hold values from 0.2 to 1
- observations: float32 [65536, 128], P(('wide', 'narrow')), may hold values from -6 to 6
- train_codes: int32 [65536], P(('wide', 'narrow')), may hold values from 0 to 1048575
- length_scales: float32 [10], replicated, may hold values from 0.03 to 0.3
- signal: float32 [1], replicated, may hold values from 0.03 to 0.1
- cand_codes: int32 [32768], P('wide'), may hold values from 0 to 1048575
Outputs:
- coefficients: float32 [65536, 128], P(('wide', 'narrow'))
- means: float32 [32768, 128], P(('wide', 'narrow'))
All inputs are finite; a program needn't handle non-finite values.
Results may differ from a plain program's by a relative error of at most 0.0003.
Values sent between devices are 32-bit elements; how exact they have to be, the bound alone decides.
No kernel may reach another device: no remote copies, remote signals or barrier semaphores. Data moves between devices by JAX's collectives and lax.ppermute only.
A program may use at most 128 MiB of HBM per device.

v0:
```python
import jax
import jax.numpy as jnp
from jax import lax
from jax.sharding import PartitionSpec as P

DIGITS = 10
RADIX = 4


def decode(codes):
    columns = []
    for place in range(DIGITS):
        columns.append((codes // RADIX**place % RADIX).astype(jnp.float32))
    return jnp.stack(columns, axis=1)


def kernel_block(left_digits, right_digits, length_scales, signal):
    total = jnp.zeros((left_digits.shape[0], right_digits.shape[0]), jnp.float32)
    for place in range(DIGITS):
        differ = left_digits[:, place][:, None] - right_digits[:, place][None, :]
        total = total + length_scales[place] * differ * differ
    return signal[0] * jnp.exp(-total)


def rotate_scale(projected, values_here, task_basis, task_values, noise):
    high = lax.Precision.HIGHEST
    rotated = jnp.dot(projected, task_basis, precision=high, preferred_element_type=jnp.float32)
    scaled = rotated / (values_here[:, None] * task_values[None, :] + noise[0])
    return jnp.dot(scaled, task_basis.T, precision=high, preferred_element_type=jnp.float32)


def local(
    basis,
    conf_values,
    task_basis,
    task_values,
    noise,
    observations,
    train_codes,
    length_scales,
    signal,
    cand_codes,
):
    high = lax.Precision.HIGHEST
    rows_all = lax.all_gather(observations, "narrow", axis=0, tiled=True)
    partial_value = lax.dot_general(
        basis,
        rows_all,
        (((0,), (0,)), ((), ())),
        precision=high,
        preferred_element_type=jnp.float32,
    )
    projected = lax.psum(partial_value, "wide")
    back = rotate_scale(projected, conf_values, task_basis, task_values, noise)
    coefficients = lax.psum_scatter(
        jnp.dot(basis, back, precision=high, preferred_element_type=jnp.float32),
        "narrow",
        scatter_dimension=0,
        tiled=True,
    )
    task_kernel = jnp.dot(
        task_basis * task_values[None, :],
        task_basis.T,
        precision=high,
        preferred_element_type=jnp.float32,
    )
    weighted = jnp.dot(
        coefficients, task_kernel, precision=high, preferred_element_type=jnp.float32
    )
    cand_digits = decode(cand_codes)
    code_values = train_codes.astype(jnp.float32)
    weight_piece = lax.all_gather(weighted, "wide", axis=0, tiled=True)
    code_piece = lax.all_gather(code_values, "wide", axis=0, tiled=True)
    cross = kernel_block(cand_digits, decode(code_piece.astype(jnp.int32)), length_scales, signal)
    totals = jnp.dot(cross, weight_piece, precision=high, preferred_element_type=jnp.float32)
    means = lax.psum_scatter(totals, "narrow", scatter_dimension=0, tiled=True)
    return (coefficients, means)


def solution(mesh):
    return jax.shard_map(
        local,
        mesh=mesh,
        in_specs=(
            P("wide", "narrow"),
            P("narrow"),
            P(),
            P(),
            P(),
            P(("wide", "narrow"), None),
            P(("wide", "narrow")),
            P(),
            P(),
            P("wide"),
        ),
        out_specs=(P(("wide", "narrow"), None), P(("wide", "narrow"), None)),
        check_vma=False,
    )
```

profile of v0, /device:TPU:32, one launch (start us, length us, event | category | flops | bytes accessed | tf_op | source)
XLA Modules:
  0.0 598.9 jit_solution(4413570675991483311)
XLA Ops:
  7.2 0.0 copy-start
  7.2 0.0 copy-start.5
  7.2 0.0 copy-start.6
  7.2 0.0 all-gather.4.cloned.1.call-start
  7.2 0.7 all-gather.4.cloned.1.call-update
  7.9 0.0 all-reduce.2.cloned.1.call-start
  8.0 67.5 %all-gather.4.cloned.1.call-done = f32[4096,128]{1,0:T(8,128)} async-done(((f32[256,128]{1,0:T(8,128)}), f32[4096,128]{1,0:T(8,128)}) %all-gather.4.cloned.1.call-update) | async-done | bytes 2097168 | tf_op jit(solution)/shard_map/all_gather | solution.py:45
  75.5 16.5 %fusion.121 = f32[512,128]{1,0:T(8,128)} fusion(f32[4096,512]{1,0:T(8,128)} %param.10, f32[4096,128]{1,0:T(8,128)} %all-gather.4.cloned.1.call-done), kind=kOutput, calls=%fused_computation.248 | convolution fusion | flops 3221225472 | bytes 10747904 | tf_op jit(solution)/shard_map/dot_general | solution.py:46
  92.0 0.0 copy-start.4
  92.0 0.0 copy-start.2
  92.0 0.0 copy-start.3
  92.0 0.0 all-reduce.2.cloned.1.call-update
  92.0 0.0 reduce-scatter.3.cloned.1.call-start
  92.7 155.8 %all-reduce.2.cloned.1.call-done = f32[512,128]{1,0:T(8,128)} async-done(((f32[512,128]{1,0:T(8,128)}), f32[512,128]{1,0:T(8,128)}) %all-reduce.2.cloned.1.call-update) | async-done | bytes 262160 | tf_op jit(solution)/shard_map/psum | solution.py:53
  248.5 0.0 copy-done
  248.5 0.0 copy-done.5
  248.5 0.0 copy-done.6
  248.5 1.3 convolution_divide_fusion
  249.8 0.4 fusion.122
  250.2 12.7 %convolution_bitcast_fusion = f32[4096,128]{0,1:T(8,128)} fusion(f32[512,128]{1,0:T(8,128)S(1)} %fusion.122, f32[4096,512]{1,0:T(8,128)} %param.10), kind=kOutput, calls=%fused_computation.54 | convolution fusion | flops 3221225472 | bytes 10747904 | tf_op jit(solution)/shard_map/dot_general | solution.py:56
  262.9 0.0 reduce-scatter.3.cloned.1.call-update
  262.9 0.0 all-gather.6.cloned.1.call-start
  263.0 0.3 fusion.45
  263.2 84.3 %reduce-scatter.3.cloned.1.call-done = f32[256,128]{0,1:T(8,128)} async-done(((f32[4096,128]{0,1:T(8,128)}), f32[256,128]{0,1:T(8,128)}) %reduce-scatter.3.cloned.1.call-update) | async-done | bytes 131088 | tf_op jit(solution)/shard_map/reduce_scatter | solution.py:55
  347.6 1.9 fusion.123
  349.5 0.0 all-gather.6.cloned.1.call-update
  349.6 0.0 reduce-scatter.5.cloned.1.call-start
  350.3 0.0 copy-done.4
  350.3 38.9 %all-gather = f32[16,1,256]{2,1,0:T(1,128)S(1)} all-gather(f32[1,1,256]{2,1,0:T(1,128)S(1)} %bitcast.32), channel_id=1, replica_groups=mesh['wide'=16,'narrow'=16] {'wide'}, dimensions={0}, use_global_device_ids=true | all-gather | bytes 17408 | tf_op jit(solution)/shard_map/all_gather | solution.py:73
  389.2 0.0 copy-done.2
  389.2 0.7 fusion.120
  389.9 0.0 copy-done.3
  389.9 0.1 fusion.84
  390.0 0.1 fusion.48
  390.1 44.7 %all-gather.6.cloned.1.call-done = f32[4096,128]{1,0:T(8,128)} async-done(((f32[256,128]{1,0:T(8,128)}), f32[4096,128]{1,0:T(8,128)}) %all-gather.6.cloned.1.call-update) | async-done | bytes 2097168 | tf_op jit(solution)/shard_map/all_gather | solution.py:72
  434.8 0.0 copy-start.1
  434.8 79.5 %fusion.12 = f32[2048,128]{1,0:T(8,128)} fusion(f32[4096,128]{1,0:T(8,128)} %all-gather.6.cloned.1.call-done, f32[4096]{0:T(1024)S(1)} %get-tuple-element.14, f32[2048]{0:T(1024)S(1)} %get-tuple-element.25, f32[]{:T(128)} %bitcast.14, f32[4096]{0:T(1024)S(1)} %get-tuple-element.10, f32[2048]{0:T(1024)S(1)} %get-tuple-element.20, f32[]{:T(128)} %bitcast.13, ...), kind=kOutput, calls=%fused_computation.22 | convolution fusion | flops 13228834816 | bytes 3391532 | tf_op jit(solution)/shard_map/dot_general | solution.py:75
  514.3 0.0 reduce-scatter.5.cloned.1.call-update
  514.3 0.0 copy-done.1
  514.3 0.8 copy.13
  515.1 77.3 %reduce-scatter.5.cloned.1.call-done = f32[128,128]{1,0:T(8,128)} async-done(((f32[2048,128]{1,0:T(8,128)}), f32[128,128]{1,0:T(8,128)}) %reduce-scatter.5.cloned.1.call-update) | async-done | bytes 65552 | tf_op jit(solution)/shard_map/reduce_scatter | solution.py:76
  (2 shorter events, 0.0 us)
Async XLA Ops:
  7.2 241.3 %copy-start = (f32[128,128]{1,0:T(8,128)S(1)}, f32[128,128]{1,0:T(8,128)}, u32[]{:S(2)}) copy-start(f32[128,128]{1,0:T(8,128)} %param.12) | copy-start | bytes 196612
  7.2 241.3 %copy-start.5 = (f32[128]{0:T(128)S(1)}, f32[128]{0:T(128)}, u32[]{:S(2)}) copy-start(f32[128]{0:T(128)} %param.13) | copy-start | bytes 1540
  7.2 241.3 %copy-start.6 = (f32[512]{0:T(512)S(1)}, f32[512]{0:T(512)}, u32[]{:S(2)}) copy-start(f32[512]{0:T(512)} %param.11) | copy-start | bytes 6148
  7.2 68.3 %all-gather.4.cloned.1.call-start = ((), (), s32[]{:S(2)}) async-start(), calls=%async_computation.2 | async-start | bytes 2228224 | tf_op jit(solution)/shard_map/all_gather | solution.py:45
  7.9 240.6 %all-reduce.2.cloned.1.call-start = ((), (), s32[]{:S(2)}) async-start(), calls=%async_computation.3 | async-start | bytes 524288 | tf_op jit(solution)/shard_map/psum | solution.py:53
  92.0 258.3 %copy-start.4 = (s32[256]{0:T(256)S(1)}, s32[256]{0:T(256)}, u32[]{:S(2)}) copy-start(s32[256]{0:T(256)} %param.16) | copy-start | bytes 3076
  92.0 297.2 %copy-start.2 = (f32[10]{0:T(128)S(1)}, f32[10]{0:T(128)}, u32[]{:S(2)}) copy-start(f32[10]{0:T(128)} %param.17) | copy-start | bytes 124
  92.0 297.9 %copy-start.3 = (s32[2048]{0:T(1024)S(1)}, s32[2048]{0:T(1024)}, u32[]{:S(2)}) copy-start(s32[2048]{0:T(1024)} %param.19) | copy-start | bytes 24580
  92.0 255.6 %reduce-scatter.3.cloned.1.call-start = ((), (), s32[]{:S(2)}) async-start(), calls=%async_computation.4 | async-start | bytes 2228224 | tf_op jit(solution)/shard_map/reduce_scatter | solution.py:55
  262.9 171.9 %all-gather.6.cloned.1.call-start = ((), (), s32[]{:S(2)}) async-start(), calls=%async_computation.5 | async-start | bytes 2228224 | tf_op jit(solution)/shard_map/all_gather | solution.py:72
  349.6 242.8 %reduce-scatter.5.cloned.1.call-start = ((), (), s32[]{:S(2)}) async-start(), calls=%async_computation.6 | async-start | bytes 1114112 | tf_op jit(solution)/shard_map/reduce_scatter | solution.py:76
  434.8 79.5 %copy-start.1 = (f32[256,128]{0,1:T(8,128)S(1)}, f32[256,128]{0,1:T(8,128)}, u32[]{:S(2)}) copy-start(f32[256,128]{0,1:T(8,128)} %reduce-scatter.3.cloned.1.call-done) | copy-start | bytes 393220
Sparse Core Ops, SparseCore 0:
  10.8 64.6 all-gather.3
  92.1 156.3 all-reduce.1
  263.1 84.4 reduce-scatter.2
  349.9 84.8 all-gather.5
  514.5 77.8 reduce-scatter.4
where the time goes:
time: 601 us; the launch traced here: 599 us
  waiting for transfers between devices  430 us (72%)
  matrix products  113 us (19%)
  blocking collectives  38.9 us (6%)
  between operations  15.2 us (3%)
    psum x1, waiting for transfers between devices, local(): projected = lax.psum(partial_value, 'wide')  156 us
    reduce_scatter x1, waiting for transfers between devices, local(): lax.psum_scatter(jnp.dot(basis, back, precision=high, preferred_element_t...  84.3 us
    dot_general x1, matrix products, local(): jnp.dot(cross, weight_piece, precision=high, preferred_element_type=jnp.f...  79.5 us
    reduce_scatter x1, waiting for transfers between devices, local(): means = lax.psum_scatter(totals, 'narrow', scatter_dimension=0, tiled=True)  77.3 us
    all_gather x1, waiting for transfers between devices, local(): rows_all = lax.all_gather(observations, 'narrow', axis=0, tiled=True)  67.5 us
    all_gather x1, waiting for transfers between devices, local(): weight_piece = lax.all_gather(weighted, 'wide', axis=0, tiled=True)  44.7 us
    all_gather x1, blocking collectives, local(): code_piece = lax.all_gather(code_values, 'wide', axis=0, tiled=True)  38.9 us
    dot_general x1, matrix products, local(): lax.dot_general(basis, rows_all, (((0,), (0,)), ((), ())), precision=high...  16.5 us
  transfers between devices with their start and end apart: 5, of which 5 were waited for; matrix products, arithmetic and copies ran while one was open for 0% of the time, Pallas kernels for 0%

commit v1 on v0

v1 whole, which is shorter than its diff:
```python
import functools
import math

import jax
import jax.numpy as jnp
from jax import lax
from jax.experimental import pallas as pl
from jax.experimental.pallas import tpu as pltpu
from jax.sharding import PartitionSpec as P

F32 = jnp.float32
BF16 = jnp.bfloat16
VM = pltpu.VMEM
MIB = 1 << 20


def split(x):
    high = x.astype(BF16)
    return high, (x - high.astype(F32)).astype(BF16)


def mul(a, b, dims=(((1,), (0,)), ((), ()))):
    return lax.dot_general(a, b, dims, preferred_element_type=F32)


def mul3(a, b, dims=(((1,), (0,)), ((), ()))):
    ah, al = split(a)
    bh, bl = split(b)
    return mul(ah, bh, dims) + (mul(ah, bl, dims) + mul(al, bh, dims))


NT = (((1,), (1,)), ((), ()))


def swap(value, axis, bits):
    return lax.ppermute(value, axis, [(i, i ^ bits) for i in range(16)])


def full(shape):
    return pl.BlockSpec(shape, lambda *_: (0,) * len(shape))


def params(mib):
    return pltpu.CompilerParams(vmem_limit_bytes=mib * MIB)


def halves_kernel(x, high, low):
    h, l = split(x[...])
    high[...] = h
    low[...] = l


def halves(basis):
    rows, columns = basis.shape
    block = pl.BlockSpec((512, columns), lambda i: (i, 0))
    return pl.pallas_call(
        halves_kernel,
        grid=(rows // 512,),
        in_specs=[block],
        out_specs=[block, block],
        out_shape=[jax.ShapeDtypeStruct(basis.shape, BF16)] * 2,
        compiler_params=params(8),
        cost_estimate=pl.CostEstimate(flops=0, bytes_accessed=16 * MIB, transcendentals=0),
        name="basis_halves",
    )(basis)


def project_kernel(where, high, low, task_basis, *refs):
    blocks, out = refs[:8], refs[8]
    me = where[0]
    total = jnp.zeros(out.shape, F32)
    for group in range(8):
        for far in range(2):
            slot = (group % 4) * 2 + group // 4 + far * 8
            rows = pl.ds(pl.multiple_of((me ^ slot) * 256, 256), 256)
            oh, ol = split(blocks[group][far, 0:128, :])
            bh = high[rows, :]
            both = mul(jnp.concatenate([oh, ol], axis=0), bh)
            total = total + both[:128] + (both[128:] + mul(oh, low[rows, :]))
    out[...] = mul3(task_basis[...].T, total)


def project(where, high, low, task_basis, blocks):
    return pl.pallas_call(
        project_kernel,
        in_specs=[pl.BlockSpec(memory_space=pltpu.SMEM)] + [pl.BlockSpec(memory_space=VM)] * 11,
        out_specs=pl.BlockSpec(memory_space=VM),
        out_shape=jax.ShapeDtypeStruct((128, high.shape[1]), F32),
        compiler_params=params(24),
        cost_estimate=pl.CostEstimate(flops=6 * 4096 * 512 * 128, bytes_accessed=10 * MIB, transcendentals=0),
        name="project",
    )(where, high, low, task_basis, *blocks)


def scale_kernel(where, noise, pieces, conf_values, task_values, out):
    rows = pl.ds(pl.multiple_of(where[1] * 8, 8), 8)
    total = jnp.sum(pieces[...], axis=0)
    scaled = total / (conf_values[...] * task_values[rows, :] + noise[0])
    out[...] = jnp.broadcast_to(scaled[None], out.shape)


def scale(where, noise, pieces, conf_values, task_values):
    smem = pl.BlockSpec(memory_space=pltpu.SMEM)
    return pl.pallas_call(
        scale_kernel,
        in_specs=[smem, smem] + [pl.BlockSpec(memory_space=VM)] * 3,
        out_specs=pl.BlockSpec(memory_space=VM),
        out_shape=jax.ShapeDtypeStruct(pieces.shape, F32),
        compiler_params=params(4),
        name="scale",
    )(where, noise, pieces, conf_values, task_values)


def expand_kernel(where, high, low, task_basis, scaled, *outs):
    me = where[0]
    back = mul3(scaled[...].T, task_basis[...], NT)
    kh, kl = split(back)
    wide = jnp.concatenate([kh, kl], axis=1)
    for group in (5, 6, 7, 4, 1, 2, 3, 0):
        for far in range(2):
            slot = (group % 4) * 2 + group // 4 + far * 8
            rows = pl.ds(pl.multiple_of((me ^ slot) * 256, 256), 256)
            both = mul(high[rows, :], wide)
            outs[group][far] = both[:, :128] + (both[:, 128:] + mul(low[rows, :], kh))


def expand(where, high, low, task_basis, scaled):
    return pl.pallas_call(
        expand_kernel,
        in_specs=[pl.BlockSpec(memory_space=pltpu.SMEM)] + [pl.BlockSpec(memory_space=VM)] * 4,
        out_specs=[pl.BlockSpec(memory_space=VM)] * 8,
        out_shape=[jax.ShapeDtypeStruct((2, 256, 128), F32)] * 8,
        compiler_params=params(24),
        cost_estimate=pl.CostEstimate(flops=6 * 4096 * 512 * 128, bytes_accessed=10 * MIB, transcendentals=0),
        name="expand",
    )(where, high, low, task_basis, scaled)


def row_digit(codes, k):
    part = (k >= 40).astype(jnp.int32) + (k >= 80).astype(jnp.int32) + (k >= 120).astype(jnp.int32)
    rest = k - 40 * part
    return part, rest & 3, lax.shift_right_logical(codes, 2 * lax.shift_right_logical(rest, 2)) & 3


def onehot_kernel(where, codes, out):
    k = lax.broadcasted_iota(jnp.int32, (128, 128), 0)
    for slot in range(16):
        row = codes[where[1] ^ slot, pl.ds(0, 1), :].astype(jnp.int32)
        _, level, digit = row_digit(jnp.broadcast_to(row, (128, 128)), k)
        hot = jnp.where(digit == level, 1.0, 0.0).astype(F32)
        out[slot * 128 : slot * 128 + 128, :] = hot.T.astype(BF16)


def onehot(where, codes):
    return pl.pallas_call(
        onehot_kernel,
        in_specs=[pl.BlockSpec(memory_space=pltpu.SMEM), pl.BlockSpec(memory_space=VM)],
        out_specs=pl.BlockSpec(memory_space=VM),
        out_shape=jax.ShapeDtypeStruct((2048, 128), BF16),
        compiler_params=params(4),
        name="candidate_levels",
    )(where, codes)


def cross_kernel(hot, codes, lengths, high, low, table):
    @pl.when(pl.program_id(0) == 0)
    def _():
        k = lax.broadcasted_iota(jnp.int32, (128, 256), 0)
        length = jnp.concatenate([lengths[...], lengths[...]], axis=1)
        for far in range(2):
            row = codes[far, 0:1, :].astype(jnp.int32)
            part, level, digit = row_digit(jnp.broadcast_to(row, (128, 256)), k)
            differ = (level - digit).astype(F32)
            value = length * differ * differ
            first = value.astype(BF16).astype(F32)
            second = (value - first).astype(BF16).astype(F32)
            third = value - first - second
            piece = jnp.where(part == 0, first, jnp.where(part == 1, second, jnp.where(part == 2, third, 0.0)))
            table[:, far * 256 : far * 256 + 256] = piece.astype(BF16)

    cross = jnp.exp2(mul(hot[...], table[...]))
    h, l = split(cross)
    high[...] = h
    low[...] = l


def cross_halves(hot, block, lengths):
    rows = hot.shape[0]
    step = 256
    out = pl.BlockSpec((step, 512), lambda i: (i, 0))
    return pl.pallas_call(
        cross_kernel,
        grid=(rows // step,),
        in_specs=[
            pl.BlockSpec((step, 128), lambda i: (i, 0)),
            pl.BlockSpec((2, 8, 256), lambda i: (0, 16, 0)),
            full((128, 128)),
        ],
        out_specs=[out, out],
        out_shape=[jax.ShapeDtypeStruct((rows, 512), BF16)] * 2,
        scratch_shapes=[pltpu.VMEM((128, 512), BF16)],
        compiler_params=params(8),
        cost_estimate=pl.CostEstimate(flops=2 * 2048 * 512 * 128, bytes_accessed=5 * MIB, transcendentals=2048 * 512),
        name="cross",
    )(hot, block, lengths)


def predict_kernel(near, other, h0, l0, h1, l1, *refs):
    total, out, wide = (refs[0] if len(refs) == 3 else None), refs[-2], refs[-1]

    @pl.when(pl.program_id(0) == 0)
    def _():
        for place, ref in enumerate((near, other)):
            for far in range(2):
                rows = pl.ds(place * 512 + far * 256, 256)
                wh, wl = split(ref[far])
                wide[rows, 0:128] = wh
                wide[rows, 128:256] = wl

    both = mul(h0[...], wide[0:512, :]) + mul(h1[...], wide[512:1024, :])
    rest = mul(l0[...], wide[0:512, 0:128]) + mul(l1[...], wide[512:1024, 0:128])
    value = both[:, :128] + (both[:, 128:] + rest)
    out[...] = value if total is None else total[...] + value


def predict(near, other, cross0, cross1, total, first, count):
    step = 256
    base = first // step
    block = pl.BlockSpec((step, 512), lambda i: (base + i, 0))
    out = pl.BlockSpec((step, 128), lambda i: (i, 0))
    extra, extra_specs = ([], []) if total is None else ([total], [pl.BlockSpec((step, 128), lambda i: (base + i, 0))])
    return pl.pallas_call(
        predict_kernel,
        grid=(count // step,),
        in_specs=[full((2, 256, 128))] * 2 + [block] * 4 + extra_specs,
        out_specs=out,
        out_shape=jax.ShapeDtypeStruct((count, 128), F32),
        scratch_shapes=[pltpu.VMEM((1024, 256), BF16)],
        compiler_params=params(10),
        cost_estimate=pl.CostEstimate(flops=6 * count * 1024 * 128, bytes_accessed=count * 4096 + count * 1024, transcendentals=0),
        name="predict",
    )(near, other, *cross0, *cross1, *extra)


def finish_kernel(signal, a, b, c, d, task_basis, task_values, out):
    kernel = mul3(task_basis[...] * task_values[...], task_basis[...], NT)
    out[...] = signal[0] * mul3(a[...] + b[...] + c[...] + d[...], kernel)


def finish(signal, parts, task_basis, task_values):
    return pl.pallas_call(
        finish_kernel,
        in_specs=[pl.BlockSpec(memory_space=pltpu.SMEM)] + [pl.BlockSpec(memory_space=VM)] * 6,
        out_specs=pl.BlockSpec(memory_space=VM),
        out_shape=jax.ShapeDtypeStruct((128, 128), F32),
        compiler_params=params(4),
        name="finish",
    )(signal, *parts, task_basis, task_values)


def local(
    basis,
    conf_values,
    task_basis,
    task_values,
    noise,
    observations,
    train_codes,
    length_scales,
    signal,
    cand_codes,
):
    n = lax.axis_index("narrow").astype(jnp.int32)
    w = lax.axis_index("wide").astype(jnp.int32)
    where = jnp.stack([n, w])
    high, low = halves(basis)

    own = jnp.concatenate(
        [observations.T, jnp.broadcast_to(train_codes.astype(F32)[None], (8, 256))], axis=0
    )
    pair = jnp.stack([own, swap(own, "narrow", 8)])
    near = [pair] + [swap(pair, "narrow", 2 * d) for d in (1, 2, 3)]
    other = [swap(block, "narrow", 1) for block in near]
    blocks = near + other

    own_codes = lax.dynamic_slice(cand_codes, (n * 128,), (128,)).astype(F32)
    codes = lax.all_to_all(jnp.broadcast_to(own_codes, (16, 8, 128)), "wide", 0, 0)
    hot = onehot(where, codes)
    exponents = jnp.repeat(length_scales * (-1.0 / math.log(2.0)), 4)
    exponents = jnp.concatenate([exponents, exponents, exponents, jnp.zeros((8,), F32)])
    lengths = jnp.broadcast_to(exponents[:, None], (128, 128))
    crosses = [cross_halves(hot, block, lengths) for block in blocks]

    rotated = project(where, high, low, task_basis, blocks)
    pieces = lax.all_to_all(rotated.reshape(16, 8, -1), "wide", 0, 0)
    scaled = scale(where, noise, pieces, conf_values[None], task_values[:, None])
    scaled = lax.all_to_all(scaled, "wide", 0, 0).reshape(128, -1)

    parts = expand(where, high, low, task_basis, scaled)
    sums = {}
    for d in (1, 2, 3, 0):
        sums[d] = parts[d] + swap(parts[4 + d], "narrow", 1)
    total = sums[0]
    for d in (1, 2, 3):
        total = total + swap(sums[d], "narrow", 2 * d)
    mirror = swap(total, "narrow", 8)
    total = total + mirror[::-1]
    coefficients = total[0]

    weights = [total] + [swap(total, "narrow", 2 * d) for d in (1, 2, 3)]
    others = [swap(block, "narrow", 1) for block in weights]
    means = None
    for d in (0, 1, 2):
        means = predict(weights[d], others[d], crosses[d], crosses[4 + d], means, 0, 2048)
    last = {}
    for g in (1, 2, 3, 0):
        last[g] = predict(weights[3], others[3], crosses[3], crosses[7], means, g * 512, 512)
    block = last[0]
    for g in (1, 2, 3):
        block = block + swap(last[g], "wide", 4 * g)
    quarters = block.reshape(4, 128, 128)
    ends = [quarters[0]] + [swap(quarters[g], "wide", g) for g in (1, 2, 3)]
    return coefficients, finish(signal, ends, task_basis, task_values[None])


def solution(mesh):
    return jax.shard_map(
        local,
        mesh=mesh,
        in_specs=(
            P("wide", "narrow"),
            P("narrow"),
            P(),
            P(),
            P(),
            P(("wide", "narrow"), None),
            P(("wide", "narrow")),
            P(),
            P(),
            P("wide"),
        ),
        out_specs=(P(("wide", "narrow"), None), P(("wide", "narrow"), None)),
        check_vma=False,
    )
```

time: 601 us -> 185 us (0.31)
  waiting for transfers between devices: 430 us -> 60.4 us
  matrix products: 113 us -> 0 us
  starting transfers between devices: 0.2 us -> 51.6 us
  Pallas kernels: 0 us -> 43.5 us
  blocking collectives: 38.9 us -> 13.6 us
  between operations: 15.2 us -> 2.32 us
  local copies, waits for them, and re-layouts: 1.48 us -> 10.5 us
    reduce_scatter x2 -> x0, waiting for transfers between devices: 162 us -> none  [the longest x1 84.3 us: local(): lax.psum_scatter(jnp.dot(basis, back, precision=high, preferred_element_t...]
    psum x1 -> x0, waiting for transfers between devices: 156 us -> none  [local(): projected = lax.psum(partial_value, 'wide')]
    dot_general x7 -> x0, matrix products: 113 us -> none  [the longest x1 79.5 us: local(): jnp.dot(cross, weight_piece, precision=high, preferred_element_type=jnp.f...]
    all_gather x2 -> x0, waiting for transfers between devices: 112 us -> none  [the longest x1 67.5 us: local(): rows_all = lax.all_gather(observations, 'narrow', axis=0, tiled=True)]
    ppermute x0 -> x29, waiting for transfers between devices: none -> 51.4 us  [swap(): return lax.ppermute(value, axis, [(i, i ^ bits) for i in range(16)])]
    pallas_call x0 -> x21, Pallas kernels: none -> 43.5 us  [the longest x8 17.4 us: cross_halves(): pl.pallas_call(cross_kernel, grid=(rows // step,), in_specs=[pl.BlockSpec...]
    all_gather x1 -> x0, blocking collectives: 38.9 us -> none  [local(): code_piece = lax.all_gather(code_values, 'wide', axis=0, tiled=True)]
    ppermute x0 -> x29, starting transfers between devices: none -> 36.9 us  [swap(): return lax.ppermute(value, axis, [(i, i ^ bits) for i in range(16)])]
  transfers between devices with their start and end apart: 5 -> 31, of which waited for: 5 -> 16; matrix products, arithmetic and copies ran while one was open for 0% -> 1% of each run, Pallas kernels for 0% -> 19%
where the time goes in v1:
time: 185 us; the launch traced here: 184 us
  waiting for transfers between devices  60.4 us (33%)
  starting transfers between devices  51.6 us (28%)
  Pallas kernels  43.5 us (24%)
  blocking collectives  13.6 us (7%)
  local copies, waits for them, and re-layouts  10.5 us (6%)
  between operations  2.32 us (1%)
  other arithmetic  1.9 us (1%)
    ppermute x29, waiting for transfers between devices, swap(): return lax.ppermute(value, axis, [(i, i ^ bits) for i in range(16)])  51.4 us
    ppermute x29, starting transfers between devices, swap(): return lax.ppermute(value, axis, [(i, i ^ bits) for i in range(16)])  36.9 us
    pallas_call x8, Pallas kernels, cross_halves(): pl.pallas_call(cross_kernel, grid=(rows // step,), in_specs=[pl.BlockSpec...  17.4 us
    pallas_call x7, Pallas kernels, predict(): pl.pallas_call(predict_kernel, grid=(count // step,), in_specs=[full((2,...  15.9 us
    all_to_all x1, blocking collectives, local(): scaled = lax.all_to_all(scaled, 'wide', 0, 0).reshape(128, -1)  13.6 us
    all_to_all x1, starting transfers between devices, local(): pieces = lax.all_to_all(rotated.reshape(16, 8, -1), 'wide', 0, 0)  9.54 us
    all_to_all x1, waiting for transfers between devices, local(): pieces = lax.all_to_all(rotated.reshape(16, 8, -1), 'wide', 0, 0)  9.07 us
    unnamed x19, local copies, waits for them, and re-layouts  8.79 us
  transfers between devices with their start and end apart: 31, of which 16 were waited for; matrix products, arithmetic and copies ran while one was open for 1% of the time, Pallas kernels for 19%

profile of v1, /device:TPU:32, one launch (start us, length us, event | category | flops | bytes accessed | tf_op | source)
XLA Modules:
  0.0 183.8 jit_solution(10646544921006601580)
XLA Ops:
  0.6 1.0 copy.14
  2.4 6.4 %collective-permute-start = (f32[136,256]{1,0:T(8,128)S(1)}, f32[136,256]{1,0:T(8,128)S(1)}, u32[]{:S(2)}, u32[]{:S(2)}) collective-permute-start(f32[136,256]{1,0:T(8,128)S(1)} %get-tuple-element.59), channel_id=1, source_target_pairs={{0,8},{1,9},{2,10},{3,11},{4,12},{5,13},{6,14},{7,15},{8,0},{9,1},... | collective-permute-start | bytes 417800 | tf_op jit(solution)/shard_map/ppermute | solution.py:36
  8.7 6.7 %collective-permute-done = f32[136,256]{1,0:T(8,128)S(1)} collective-permute-done((f32[136,256]{1,0:T(8,128)S(1)}, f32[136,256]{1,0:T(8,128)S(1)}, u32[]{:S(2)}, u32[]{:S(2)}) %collective-permute-start) | collective-permute-done | bytes 139296 | tf_op jit(solution)/shard_map/ppermute | solution.py:36
  15.5 1.7 collective-permute-start.1
  17.1 2.9 %collective-permute-start.2 = (f32[2,136,256]{2,1,0:T(8,128)S(1)}, f32[2,136,256]{2,1,0:T(8,128)S(1)}, u32[]{:S(2)}, u32[]{:S(2)}) collective-permute-start(f32[2,136,256]{2,1,0:T(8,128)S(1)} %pad_maximum_fusion.refs_0_.codes), channel_id=1, source_target_pairs={{0,4},{1,5},{2,6},{3,7},{4,0},{5,1},{6,2},{7,3},{8,12},{9,13},{10,... | collective-permute-start | bytes 835592 | tf_op jit(solution)/shard_map/ppermute | solution.py:36
  20.2 3.1 %collective-permute-done.1.refs_1_.codes = f32[2,136,256]{2,1,0:T(8,128)S(1)} collective-permute-done((f32[2,136,256]{2,1,0:T(8,128)S(1)}, f32[2,136,256]{2,1,0:T(8,128)S(1)}, u32[]{:S(2)}, u32[]{:S(2)}) %collective-permute-start.1) | collective-permute-done | bytes 278560 | tf_op jit(solution)/shard_map/ppermute | solution.py:36
  23.4 5.5 %collective-permute-done.2.refs_2_.codes = f32[2,136,256]{2,1,0:T(8,128)S(1)} collective-permute-done((f32[2,136,256]{2,1,0:T(8,128)S(1)}, f32[2,136,256]{2,1,0:T(8,128)S(1)}, u32[]{:S(2)}, u32[]{:S(2)}) %collective-permute-start.2) | collective-permute-done | bytes 278560 | tf_op jit(solution)/shard_map/ppermute | solution.py:36
  28.9 2.5 %collective-permute-done.3.refs_3_.codes = f32[2,136,256]{2,1,0:T(8,128)S(1)} collective-permute-done((f32[2,136,256]{2,1,0:T(8,128)S(1)}, f32[2,136,256]{2,1,0:T(8,128)S(1)}, u32[]{:S(2)}, u32[]{:S(2)}) %collective-permute-start.3) | collective-permute-done | bytes 278560 | tf_op jit(solution)/shard_map/ppermute | solution.py:36
  31.5 3.4 %copy-done.4 = f32[4096,512]{1,0:T(8,128)S(1)} copy-done((f32[4096,512]{1,0:T(8,128)S(1)}, f32[4096,512]{1,0:T(8,128)}, u32[]{:S(2)}) %copy-start.4) | copy-done | bytes 8388632
  34.9 1.2 basis_halves.1
  36.2 3.3 %project.1 = f32[128,512]{1,0:T(8,128)} custom-call(s32[2]{0:T(128)S(1)} %pad_add_fusion.where, bf16[4096,512]{1,0:T(8,128)(2,1)S(1)} %get-tuple-element.28.high, bf16[4096,512]{1,0:T(8,128)(2,1)S(1)} %get-tuple-element.29.low, f32[128,128]{1,0:T(8,128)S(1)} %copy-done.5, f32[2,136,256]{2,1,0:T(8,128)S(1)} %pad_maximum_fusion.refs_0_.codes, ...), custom_call_target="tpu_custom_call" | custom-call | flops 1610612736 | bytes 10485760 | tf_op jit(solution)/shard_map/project/pallas_call | solution.py:84
  39.5 9.5 %all-to-all-start = ((f32[16,8,512]{2,1,0:T(8,128)}), f32[16,8,512]{2,1,0:T(8,128)S(1)}, u32[]{:S(2)}, u32[]{:S(2)}) async-start(f32[16,8,512]{2,1,0:T(8,128)} %bitcast.5), calls=%async_computation | async-start | bytes 524288 | tf_op jit(solution)/shard_map/all_to_all | solution.py:295
  49.8 9.1 %all-to-all-done.pieces = f32[16,8,512]{2,1,0:T(8,128)S(1)} async-done(((f32[16,8,512]{2,1,0:T(8,128)}), f32[16,8,512]{2,1,0:T(8,128)S(1)}, u32[]{:S(2)}, u32[]{:S(2)}) %all-to-all-start) | async-done | bytes 262176 | tf_op jit(solution)/shard_map/all_to_all | solution.py:295
  59.5 13.6 %all_to_all.15 = f32[16,8,512]{2,1,0:T(8,128)S(1)} all-to-all(f32[16,8,512]{2,1,0:T(8,128)S(1)} %scale.1), channel_id=1, replica_groups=mesh['wide'=16,'narrow'=16] {'wide'}, dimensions={0} | all-to-all | bytes 524288 | tf_op jit(solution)/shard_map/all_to_all | solution.py:297
  73.2 2.2 %copy-done.1 = bf16[4096,512]{1,0:T(8,128)(2,1)S(1)} copy-done((bf16[4096,512]{1,0:T(8,128)(2,1)S(1)}, bf16[4096,512]{1,0:T(8,128)(2,1)}, u32[]{:S(2)}) %copy-start.1) | copy-done | bytes 4194328
  75.4 2.2 %copy-done.3 = bf16[4096,512]{1,0:T(8,128)(2,1)S(1)} copy-done((bf16[4096,512]{1,0:T(8,128)(2,1)S(1)}, bf16[4096,512]{1,0:T(8,128)(2,1)}, u32[]{:S(2)}) %copy-start.3) | copy-done | bytes 4194328
  77.6 3.3 %expand.1 = (f32[2,256,128]{2,1,0:T(8,128)S(1)}, f32[2,256,128]{2,1,0:T(8,128)S(1)}, f32[2,256,128]{2,1,0:T(8,128)S(1)}, f32[2,256,128]{2,1,0:T(8,128)S(1)}, f32...) custom-call(s32[2]{0:T(128)S(1)} %pad_add_fusion.where, ...), custom_call_target="tpu_custom_call" | custom-call | flops 1610612736 | bytes 10485760 | tf_op jit(solution)/shard_map/expand/pallas_call | solution.py:128
  82.8 1.8 collective-permute-start.12
  84.7 3.0 %collective-permute-start.14 = (f32[2,256,128]{2,1,0:T(8,128)S(1)}, f32[2,256,128]{2,1,0:T(8,128)S(1)}, u32[]{:S(2)}, u32[]{:S(2)}) collective-permute-start(f32[2,256,128]{2,1,0:T(8,128)S(1)} %add.41), channel_id=1, source_target_pairs={{0,6},{1,7},{2,4},{3,5},{4,2},{5,3},{6,0},{7,1},{8,14},{9,15},{10,... | collective-permute-start | bytes 786440 | tf_op jit(solution)/shard_map/ppermute | solution.py:36
  87.7 4.2 %collective-permute-done.10 = f32[2,256,128]{2,1,0:T(8,128)S(1)} collective-permute-done((f32[2,256,128]{2,1,0:T(8,128)S(1)}, f32[2,256,128]{2,1,0:T(8,128)S(1)}, u32[]{:S(2)}, u32[]{:S(2)}) %collective-permute-start.10) | collective-permute-done | bytes 262176 | tf_op jit(solution)/shard_map/ppermute | solution.py:36
  91.9 4.6 %collective-permute-done.12 = f32[2,256,128]{2,1,0:T(8,128)S(1)} collective-permute-done((f32[2,256,128]{2,1,0:T(8,128)S(1)}, f32[2,256,128]{2,1,0:T(8,128)S(1)}, u32[]{:S(2)}, u32[]{:S(2)}) %collective-permute-start.12) | collective-permute-done | bytes 262176 | tf_op jit(solution)/shard_map/ppermute | solution.py:36
  96.6 2.8 %collective-permute-done.14 = f32[2,256,128]{2,1,0:T(8,128)S(1)} collective-permute-done((f32[2,256,128]{2,1,0:T(8,128)S(1)}, f32[2,256,128]{2,1,0:T(8,128)S(1)}, u32[]{:S(2)}, u32[]{:S(2)}) %collective-permute-start.14) | collective-permute-done | bytes 262176 | tf_op jit(solution)/shard_map/ppermute | solution.py:36
  99.5 5.2 %collective-permute-start.15 = (f32[2,256,128]{2,1,0:T(8,128)S(1)}, f32[2,256,128]{2,1,0:T(8,128)S(1)}, u32[]{:S(2)}, u32[]{:S(2)}) collective-permute-start(f32[2,256,128]{2,1,0:T(8,128)S(1)} %add_add_fusion.1), channel_id=1, source_target_pairs={{0,8},{1,9},{2,10},{3,11},{4,12},{5,13},{6,14},{7,15},{8,0},{9,1},... | collective-permute-start | bytes 786440 | tf_op jit(solution)/shard_map/ppermute | solution.py:36
  106.0 5.1 %all-to-all-start.2 = ((f32[16,8,128]{2,1,0:T(8,128)}), f32[16,8,128]{2,1,0:T(8,128)S(1)}, u32[]{:S(2)}, u32[]{:S(2)}) async-start(f32[16,8,128]{2,1,0:T(8,128)} %broadcast_in_dim.30), calls=%async_computation.2 | async-start | bytes 131072 | tf_op jit(solution)/shard_map/all_to_all | solution.py:287
  111.1 5.1 %collective-permute-done.15 = f32[2,256,128]{2,1,0:T(8,128)S(1)} collective-permute-done((f32[2,256,128]{2,1,0:T(8,128)S(1)}, f32[2,256,128]{2,1,0:T(8,128)S(1)}, u32[]{:S(2)}, u32[]{:S(2)}) %collective-permute-start.15) | collective-permute-done | bytes 262176 | tf_op jit(solution)/shard_map/ppermute | solution.py:36
  116.6 4.5 %collective-permute-start.18 = (f32[2,256,128]{2,1,0:T(8,128)S(1)}, f32[2,256,128]{2,1,0:T(8,128)S(1)}, u32[]{:S(2)}, u32[]{:S(2)}) collective-permute-start(f32[2,256,128]{2,1,0:T(8,128)S(1)} %reverse_add_fusion.near), channel_id=1, source_target_pairs={{0,4},{1,5},{2,6},{3,7},{4,0},{5,1},{6,2},{7,3},{8,12},{9,13},{10,... | collective-permute-start | bytes 786440 | tf_op jit(solution)/shard_map/ppermute | solution.py:36
  122.3 2.1 %cross.14 = (bf16[2048,512]{1,0:T(8,128)(2,1)S(1)}, bf16[2048,512]{1,0:T(8,128)(2,1)S(1)}) custom-call(bf16[2048,128]{1,0:T(8,128)(2,1)S(1)} %candidate_levels.1.hot, f32[2,136,256]{2,1,0:T(8,128)S(1)} %pad_maximum_fusion.refs_0_.codes, f32[128,128]{1,0:T(8,128)S(1)} %broadcast_in_dim.32.lengths), custom_call_target="tpu_custom_call" | custom-call | flops 268435456 | bytes 5242880 | tf_op jit(solution)/shard_map/cross/pallas_call | solution.py:191
  124.5 2.2 %cross.15 = (bf16[2048,512]{1,0:T(8,128)(2,1)S(1)}, bf16[2048,512]{1,0:T(8,128)(2,1)S(1)}) custom-call(bf16[2048,128]{1,0:T(8,128)(2,1)S(1)} %candidate_levels.1.hot, f32[2,136,256]{2,1,0:T(8,128)S(1)} %collective-permute-done.4.refs_4_.codes, f32[128,128]{1,0:T(8,128)S(1)} %broadcast_in_dim.32.lengths), custom_call_target="tpu_custom_call" | custom-call | flops 268435456 | bytes 5242880 | tf_op jit(solution)/shard_map/cross/pallas_call | solution.py:191
  126.7 2.2 %cross.12 = (bf16[2048,512]{1,0:T(8,128)(2,1)S(1)}, bf16[2048,512]{1,0:T(8,128)(2,1)S(1)}) custom-call(bf16[2048,128]{1,0:T(8,128)(2,1)S(1)} %candidate_levels.1.hot, f32[2,136,256]{2,1,0:T(8,128)S(1)} %collective-permute-done.1.refs_1_.codes, f32[128,128]{1,0:T(8,128)S(1)} %broadcast_in_dim.32.lengths), custom_call_target="tpu_custom_call" | custom-call | flops 268435456 | bytes 5242880 | tf_op jit(solution)/shard_map/cross/pallas_call | solution.py:191
  128.9 2.2 %cross.10 = (bf16[2048,512]{1,0:T(8,128)(2,1)S(1)}, bf16[2048,512]{1,0:T(8,128)(2,1)S(1)}) custom-call(bf16[2048,128]{1,0:T(8,128)(2,1)S(1)} %candidate_levels.1.hot, f32[2,136,256]{2,1,0:T(8,128)S(1)} %collective-permute-done.2.refs_2_.codes, f32[128,128]{1,0:T(8,128)S(1)} %broadcast_in_dim.32.lengths), custom_call_target="tpu_custom_call" | custom-call | flops 268435456 | bytes 5242880 | tf_op jit(solution)/shard_map/cross/pallas_call | solution.py:191
  131.2 2.2 %cross.8 = (bf16[2048,512]{1,0:T(8,128)(2,1)S(1)}, bf16[2048,512]{1,0:T(8,128)(2,1)S(1)}) custom-call(bf16[2048,128]{1,0:T(8,128)(2,1)S(1)} %candidate_levels.1.hot, f32[2,136,256]{2,1,0:T(8,128)S(1)} %collective-permute-done.3.refs_3_.codes, f32[128,128]{1,0:T(8,128)S(1)} %broadcast_in_dim.32.lengths), custom_call_target="tpu_custom_call" | custom-call | flops 268435456 | bytes 5242880 | tf_op jit(solution)/shard_map/cross/pallas_call | solution.py:191
  133.3 2.2 %cross.13 = (bf16[2048,512]{1,0:T(8,128)(2,1)S(1)}, bf16[2048,512]{1,0:T(8,128)(2,1)S(1)}) custom-call(bf16[2048,128]{1,0:T(8,128)(2,1)S(1)} %candidate_levels.1.hot, f32[2,136,256]{2,1,0:T(8,128)S(1)} %collective-permute-done.5.refs_5_.codes, f32[128,128]{1,0:T(8,128)S(1)} %broadcast_in_dim.32.lengths), custom_call_target="tpu_custom_call" | custom-call | flops 268435456 | bytes 5242880 | tf_op jit(solution)/shard_map/cross/pallas_call | solution.py:191
  135.5 2.2 %cross.11 = (bf16[2048,512]{1,0:T(8,128)(2,1)S(1)}, bf16[2048,512]{1,0:T(8,128)(2,1)S(1)}) custom-call(bf16[2048,128]{1,0:T(8,128)(2,1)S(1)} %candidate_levels.1.hot, f32[2,136,256]{2,1,0:T(8,128)S(1)} %collective-permute-done.6.refs_6_.codes, f32[128,128]{1,0:T(8,128)S(1)} %broadcast_in_dim.32.lengths), custom_call_target="tpu_custom_call" | custom-call | flops 268435456 | bytes 5242880 | tf_op jit(solution)/shard_map/cross/pallas_call | solution.py:191
  137.7 2.2 %cross.9 = (bf16[2048,512]{1,0:T(8,128)(2,1)S(1)}, bf16[2048,512]{1,0:T(8,128)(2,1)S(1)}) custom-call(bf16[2048,128]{1,0:T(8,128)(2,1)S(1)} %candidate_levels.1.hot, f32[2,136,256]{2,1,0:T(8,128)S(1)} %collective-permute-done.7.refs_7_.codes, f32[128,128]{1,0:T(8,128)S(1)} %broadcast_in_dim.32.lengths), custom_call_target="tpu_custom_call" | custom-call | flops 268435456 | bytes 5242880 | tf_op jit(solution)/shard_map/cross/pallas_call | solution.py:191
  140.6 4.6 %predict.7.refs_0_ = f32[2048,128]{1,0:T(8,128)S(1)} custom-call(f32[2,256,128]{2,1,0:T(8,128)S(1)} %reverse_add_fusion.near, f32[2,256,128]{2,1,0:T(8,128)} %collective-permute-done.22.other, bf16[2048,512]{1,0:T(8,128)(2,1)S(1)} %get-tuple-element.50.h0, bf16[2048,512]{1,0:T(8,128)(2,1)S(1)} %get-tuple-element.51.l0, ...), custom_call_target="tpu_custom_call" | custom-call | flops 1610612736 | bytes 10485760 | tf_op jit(solution)/shard_map/predict/pallas_call | solution.py:232
  145.2 3.6 %predict.8.refs_0_ = f32[2048,128]{1,0:T(8,128)S(1)} custom-call(f32[2,256,128]{2,1,0:T(8,128)S(1)} %collective-permute-done.20.near, f32[2,256,128]{2,1,0:T(8,128)S(1)} %collective-permute-done.21.other, bf16[2048,512]{1,0:T(8,128)(2,1)S(1)} %get-tuple-element.46.h0, bf16[2048,512]{1,0:T(8,128)(2,1)S(1)} %get-tuple-element.47.l0, ...), custom_call_target="tpu_custom_call" | custom-call | flops 1610612736 | bytes 10485760 | tf_op jit(solution)/shard_map/predict/pallas_call | solution.py:232
  148.9 3.6 %predict.9.refs_0_ = f32[2048,128]{1,0:T(8,128)S(1)} custom-call(f32[2,256,128]{2,1,0:T(8,128)S(1)} %collective-permute-done.18.near, f32[2,256,128]{2,1,0:T(8,128)S(1)} %collective-permute-done.19.other, bf16[2048,512]{1,0:T(8,128)(2,1)S(1)} %get-tuple-element.42.h0, bf16[2048,512]{1,0:T(8,128)(2,1)S(1)} %get-tuple-element.43.l0, ...), custom_call_target="tpu_custom_call" | custom-call | flops 1610612736 | bytes 10485760 | tf_op jit(solution)/shard_map/predict/pallas_call | solution.py:232
  152.5 1.0 predict.11
  155.5 2.4 %collective-permute-start.24 = (f32[512,128]{1,0:T(8,128)S(1)}, f32[512,128]{1,0:T(8,128)S(1)}, u32[]{:S(2)}, u32[]{:S(2)}) collective-permute-start(f32[512,128]{1,0:T(8,128)S(1)} %predict.12), channel_id=1, source_target_pairs={{0,128},{16,144},{32,160},{48,176},{64,192},{80,208},{96,224},{112... | collective-permute-start | bytes 786440 | tf_op jit(solution)/shard_map/ppermute | solution.py:36
  158.9 1.8 collective-permute-start.25
  161.4 1.0 predict.10
  162.7 6.2 %collective-permute-done.24 = f32[512,128]{1,0:T(8,128)S(1)} collective-permute-done((f32[512,128]{1,0:T(8,128)S(1)}, f32[512,128]{1,0:T(8,128)S(1)}, u32[]{:S(2)}, u32[]{:S(2)}) %collective-permute-start.24) | collective-permute-done | bytes 262176 | tf_op jit(solution)/shard_map/ppermute | solution.py:36
  169.0 4.9 %collective-permute-done.25 = f32[512,128]{1,0:T(8,128)S(1)} collective-permute-done((f32[512,128]{1,0:T(8,128)S(1)}, f32[512,128]{1,0:T(8,128)S(1)}, u32[]{:S(2)}, u32[]{:S(2)}) %collective-permute-start.25) | collective-permute-done | bytes 262176 | tf_op jit(solution)/shard_map/ppermute | solution.py:36
  174.1 2.2 %collective-permute-start.27 = (f32[128,128]{1,0:T(8,128)S(1)}, f32[128,128]{1,0:T(8,128)S(1)}, u32[]{:S(2)}, u32[]{:S(2)}) collective-permute-start(f32[128,128]{1,0:T(8,128)S(1)} %get-tuple-element.55), channel_id=1, source_target_pairs={{0,32},{16,48},{32,0},{48,16},{64,96},{80,112},{96,64},{112,80},{1... | collective-permute-start | bytes 196616 | tf_op jit(solution)/shard_map/ppermute | solution.py:36
  176.2 1.3 collective-permute-start.28
  178.4 2.1 %collective-permute-done.27.c = f32[128,128]{1,0:T(8,128)S(1)} collective-permute-done((f32[128,128]{1,0:T(8,128)S(1)}, f32[128,128]{1,0:T(8,128)S(1)}, u32[]{:S(2)}, u32[]{:S(2)}) %collective-permute-start.27) | collective-permute-done | bytes 65568 | tf_op jit(solution)/shard_map/ppermute | solution.py:36
  180.5 2.3 %collective-permute-done.28.d = f32[128,128]{1,0:T(8,128)S(1)} collective-permute-done((f32[128,128]{1,0:T(8,128)S(1)}, f32[128,128]{1,0:T(8,128)S(1)}, u32[]{:S(2)}, u32[]{:S(2)}) %collective-permute-start.28) | collective-permute-done | bytes 65568 | tf_op jit(solution)/shard_map/ppermute | solution.py:36
  182.8 1.0 finish.1
  (77 shorter events, 12.0 us)
Async XLA Ops:
  2.4 13.1 %collective-permute-start = (f32[136,256]{1,0:T(8,128)S(1)}, f32[136,256]{1,0:T(8,128)S(1)}, u32[]{:S(2)}, u32[]{:S(2)}) collective-permute-start(f32[136,256]{1,0:T(8,128)S(1)} %get-tuple-element.59), channel_id=1, source_target_pairs={{0,8},{1,9},{2,10},{3,11},{4,12},{5,13},{6,14},{7,15},{8,0},{9,1},... | collective-permute-start | bytes 417800 | tf_op jit(solution)/shard_map/ppermute | solution.py:36
  15.5 7.9 %collective-permute-start.1 = (f32[2,136,256]{2,1,0:T(8,128)S(1)}, f32[2,136,256]{2,1,0:T(8,128)S(1)}, u32[]{:S(2)}, u32[]{:S(2)}) collective-permute-start(f32[2,136,256]{2,1,0:T(8,128)S(1)} %pad_maximum_fusion.refs_0_.codes), channel_id=1, source_target_pairs={{0,2},{1,3},{2,0},{3,1},{4,6},{5,7},{6,4},{7,5},{8,10},{9,11},{10,... | collective-permute-start | bytes 835592 | tf_op jit(solution)/shard_map/ppermute | solution.py:36
  17.1 11.8 %collective-permute-start.2 = (f32[2,136,256]{2,1,0:T(8,128)S(1)}, f32[2,136,256]{2,1,0:T(8,128)S(1)}, u32[]{:S(2)}, u32[]{:S(2)}) collective-permute-start(f32[2,136,256]{2,1,0:T(8,128)S(1)} %pad_maximum_fusion.refs_0_.codes), channel_id=1, source_target_pairs={{0,4},{1,5},{2,6},{3,7},{4,0},{5,1},{6,2},{7,3},{8,12},{9,13},{10,... | collective-permute-start | bytes 835592 | tf_op jit(solution)/shard_map/ppermute | solution.py:36
  20.0 11.4 %collective-permute-start.3 = (f32[2,136,256]{2,1,0:T(8,128)S(1)}, f32[2,136,256]{2,1,0:T(8,128)S(1)}, u32[]{:S(2)}, u32[]{:S(2)}) collective-permute-start(f32[2,136,256]{2,1,0:T(8,128)S(1)} %pad_maximum_fusion.refs_0_.codes), channel_id=1, source_target_pairs={{0,6},{1,7},{2,4},{3,5},{4,2},{5,3},{6,0},{7,1},{8,14},{9,15},{10,... | collective-permute-start | bytes 835592 | tf_op jit(solution)/shard_map/ppermute | solution.py:36
  20.2 15.9 %collective-permute-start.4 = (f32[2,136,256]{2,1,0:T(8,128)S(1)}, f32[2,136,256]{2,1,0:T(8,128)S(1)}, u32[]{:S(2)}, u32[]{:S(2)}) collective-permute-start(f32[2,136,256]{2,1,0:T(8,128)S(1)} %pad_maximum_fusion.refs_0_.codes), channel_id=1, source_target_pairs={{0,1},{1,0},{2,3},{3,2},{4,5},{5,4},{6,7},{7,6},{8,9},{9,8},{10,11... | collective-permute-start | bytes 835592 | tf_op jit(solution)/shard_map/ppermute | solution.py:36
  23.4 12.8 %collective-permute-start.5 = (f32[2,136,256]{2,1,0:T(8,128)S(1)}, f32[2,136,256]{2,1,0:T(8,128)S(1)}, u32[]{:S(2)}, u32[]{:S(2)}) collective-permute-start(f32[2,136,256]{2,1,0:T(8,128)S(1)} %collective-permute-done.1.refs_1_.codes), channel_id=1, source_target_pairs={{0,1},{1,0},{2,3},{3,2},{4,5},{5,4},{6,7},{7,6},{8,9},{9,8},{10,11... | collective-permute-start | bytes 835592 | tf_op jit(solution)/shard_map/ppermute | solution.py:36
  28.9 7.2 %collective-permute-start.6 = (f32[2,136,256]{2,1,0:T(8,128)S(1)}, f32[2,136,256]{2,1,0:T(8,128)S(1)}, u32[]{:S(2)}, u32[]{:S(2)}) collective-permute-start(f32[2,136,256]{2,1,0:T(8,128)S(1)} %collective-permute-done.2.refs_2_.codes), channel_id=1, source_target_pairs={{0,1},{1,0},{2,3},{3,2},{4,5},{5,4},{6,7},{7,6},{8,9},{9,8},{10,11... | collective-permute-start | bytes 835592 | tf_op jit(solution)/shard_map/ppermute | solution.py:36
  31.5 4.7 %collective-permute-start.7 = (f32[2,136,256]{2,1,0:T(8,128)S(1)}, f32[2,136,256]{2,1,0:T(8,128)S(1)}, u32[]{:S(2)}, u32[]{:S(2)}) collective-permute-start(f32[2,136,256]{2,1,0:T(8,128)S(1)} %collective-permute-done.3.refs_3_.codes), channel_id=1, source_target_pairs={{0,1},{1,0},{2,3},{3,2},{4,5},{5,4},{6,7},{7,6},{8,9},{9,8},{10,11... | collective-permute-start | bytes 835592 | tf_op jit(solution)/shard_map/ppermute | solution.py:36
  31.5 3.4 %copy-start.4 = (f32[4096,512]{1,0:T(8,128)S(1)}, f32[4096,512]{1,0:T(8,128)}, u32[]{:S(2)}) copy-start(f32[4096,512]{1,0:T(8,128)} %x.1) | copy-start | bytes 25165828
  34.8 1.3 copy-start.5
  36.1 3.5 %copy-start = (bf16[4096,512]{1,0:T(8,128)(2,1)}, bf16[4096,512]{1,0:T(8,128)(2,1)S(1)}, u32[]{:S(2)}) copy-start(bf16[4096,512]{1,0:T(8,128)(2,1)S(1)} %get-tuple-element.28.high) | copy-start | bytes 12582916
  36.1 3.4 %copy-start.2 = (bf16[4096,512]{1,0:T(8,128)(2,1)}, bf16[4096,512]{1,0:T(8,128)(2,1)S(1)}, u32[]{:S(2)}) copy-start(bf16[4096,512]{1,0:T(8,128)(2,1)S(1)} %get-tuple-element.29.low) | copy-start | bytes 12582916
  36.2 12.9 %copy-start.7 = (f32[128]{0:T(128)S(1)}, f32[128]{0:T(128)}, u32[]{:S(2)}) copy-start(f32[128]{0:T(128)} %param.13) | copy-start | bytes 1540
  36.2 22.7 %copy-start.6 = (f32[512]{0:T(512)S(1)}, f32[512]{0:T(512)}, u32[]{:S(2)}) copy-start(f32[512]{0:T(512)} %param.11) | copy-start | bytes 6148
  39.5 19.4 %all-to-all-start = ((f32[16,8,512]{2,1,0:T(8,128)}), f32[16,8,512]{2,1,0:T(8,128)S(1)}, u32[]{:S(2)}, u32[]{:S(2)}) async-start(f32[16,8,512]{2,1,0:T(8,128)} %bitcast.5), calls=%async_computation | async-start | bytes 524288 | tf_op jit(solution)/shard_map/all_to_all | solution.py:295
  73.2 2.2 %copy-start.1 = (bf16[4096,512]{1,0:T(8,128)(2,1)S(1)}, bf16[4096,512]{1,0:T(8,128)(2,1)}, u32[]{:S(2)}) copy-start(bf16[4096,512]{1,0:T(8,128)(2,1)} %copy-done) | copy-start | bytes 12582916
  75.4 2.2 %copy-start.3 = (bf16[4096,512]{1,0:T(8,128)(2,1)S(1)}, bf16[4096,512]{1,0:T(8,128)(2,1)}, u32[]{:S(2)}) copy-start(bf16[4096,512]{1,0:T(8,128)(2,1)} %copy-done.2) | copy-start | bytes 12582916
  80.8 1.6 collective-permute-start.9
  80.9 1.9 %collective-permute-start.11 = (f32[2,256,128]{2,1,0:T(8,128)S(1)}, f32[2,256,128]{2,1,0:T(8,128)S(1)}, u32[]{:S(2)}, u32[]{:S(2)}) collective-permute-start(f32[2,256,128]{2,1,0:T(8,128)S(1)} %get-tuple-element.35), channel_id=1, source_target_pairs={{0,1},{1,0},{2,3},{3,2},{4,5},{5,4},{6,7},{7,6},{8,9},{9,8},{10,11... | collective-permute-start | bytes 786440 | tf_op jit(solution)/shard_map/ppermute | solution.py:36
  81.4 3.2 %collective-permute-start.13 = (f32[2,256,128]{2,1,0:T(8,128)S(1)}, f32[2,256,128]{2,1,0:T(8,128)S(1)}, u32[]{:S(2)}, u32[]{:S(2)}) collective-permute-start(f32[2,256,128]{2,1,0:T(8,128)S(1)} %get-tuple-element.37), channel_id=1, source_target_pairs={{0,1},{1,0},{2,3},{3,2},{4,5},{5,4},{6,7},{7,6},{8,9},{9,8},{10,11... | collective-permute-start | bytes 786440 | tf_op jit(solution)/shard_map/ppermute | solution.py:36
  81.5 6.2 %collective-permute-start.8 = (f32[2,256,128]{2,1,0:T(8,128)S(1)}, f32[2,256,128]{2,1,0:T(8,128)S(1)}, u32[]{:S(2)}, u32[]{:S(2)}) collective-permute-start(f32[2,256,128]{2,1,0:T(8,128)S(1)} %get-tuple-element.31), channel_id=1, source_target_pairs={{0,1},{1,0},{2,3},{3,2},{4,5},{5,4},{6,7},{7,6},{8,9},{9,8},{10,11... | collective-permute-start | bytes 786440 | tf_op jit(solution)/shard_map/ppermute | solution.py:36
  82.5 33.9 %copy-start.8 = (f32[10]{0:T(128)S(1)}, f32[10]{0:T(128)}, u32[]{:S(2)}) copy-start(f32[10]{0:T(128)} %param.17) | copy-start | bytes 124
  82.5 9.4 %collective-permute-start.10 = (f32[2,256,128]{2,1,0:T(8,128)S(1)}, f32[2,256,128]{2,1,0:T(8,128)S(1)}, u32[]{:S(2)}, u32[]{:S(2)}) collective-permute-start(f32[2,256,128]{2,1,0:T(8,128)S(1)} %add.37), channel_id=1, source_target_pairs={{0,2},{1,3},{2,0},{3,1},{4,6},{5,7},{6,4},{7,5},{8,10},{9,11},{10,... | collective-permute-start | bytes 786440 | tf_op jit(solution)/shard_map/ppermute | solution.py:36
  82.8 13.7 %collective-permute-start.12 = (f32[2,256,128]{2,1,0:T(8,128)S(1)}, f32[2,256,128]{2,1,0:T(8,128)S(1)}, u32[]{:S(2)}, u32[]{:S(2)}) collective-permute-start(f32[2,256,128]{2,1,0:T(8,128)S(1)} %add.39), channel_id=1, source_target_pairs={{0,4},{1,5},{2,6},{3,7},{4,0},{5,1},{6,2},{7,3},{8,12},{9,13},{10,... | collective-permute-start | bytes 786440 | tf_op jit(solution)/shard_map/ppermute | solution.py:36
  84.7 14.7 %collective-permute-start.14 = (f32[2,256,128]{2,1,0:T(8,128)S(1)}, f32[2,256,128]{2,1,0:T(8,128)S(1)}, u32[]{:S(2)}, u32[]{:S(2)}) collective-permute-start(f32[2,256,128]{2,1,0:T(8,128)S(1)} %add.41), channel_id=1, source_target_pairs={{0,6},{1,7},{2,4},{3,5},{4,2},{5,3},{6,0},{7,1},{8,14},{9,15},{10,... | collective-permute-start | bytes 786440 | tf_op jit(solution)/shard_map/ppermute | solution.py:36
  99.5 16.8 %collective-permute-start.15 = (f32[2,256,128]{2,1,0:T(8,128)S(1)}, f32[2,256,128]{2,1,0:T(8,128)S(1)}, u32[]{:S(2)}, u32[]{:S(2)}) collective-permute-start(f32[2,256,128]{2,1,0:T(8,128)S(1)} %add_add_fusion.1), channel_id=1, source_target_pairs={{0,8},{1,9},{2,10},{3,11},{4,12},{5,13},{6,14},{7,15},{8,0},{9,1},... | collective-permute-start | bytes 786440 | tf_op jit(solution)/shard_map/ppermute | solution.py:36
  106.0 15.4 %all-to-all-start.2 = ((f32[16,8,128]{2,1,0:T(8,128)}), f32[16,8,128]{2,1,0:T(8,128)S(1)}, u32[]{:S(2)}, u32[]{:S(2)}) async-start(f32[16,8,128]{2,1,0:T(8,128)} %broadcast_in_dim.30), calls=%async_computation.2 | async-start | bytes 131072 | tf_op jit(solution)/shard_map/all_to_all | solution.py:287
  116.3 12.6 %collective-permute-start.20 = (f32[2,256,128]{2,1,0:T(8,128)S(1)}, f32[2,256,128]{2,1,0:T(8,128)S(1)}, u32[]{:S(2)}, u32[]{:S(2)}) collective-permute-start(f32[2,256,128]{2,1,0:T(8,128)S(1)} %reverse_add_fusion.near), channel_id=1, source_target_pairs={{0,2},{1,3},{2,0},{3,1},{4,6},{5,7},{6,4},{7,5},{8,10},{9,11},{10,... | collective-permute-start | bytes 786440 | tf_op jit(solution)/shard_map/ppermute | solution.py:36
  116.5 24.0 %collective-permute-start.22 = (f32[2,256,128]{2,1,0:T(8,128)S(1)}, f32[2,256,128]{2,1,0:T(8,128)}, u32[]{:S(2)}, u32[]{:S(2)}) collective-permute-start(f32[2,256,128]{2,1,0:T(8,128)S(1)} %reverse_add_fusion.near), channel_id=1, source_target_pairs={{0,1},{1,0},{2,3},{3,2},{4,5},{5,4},{6,7},{7,6},{8,9},{9,8},{10,11... | collective-permute-start | bytes 786440 | tf_op jit(solution)/shard_map/ppermute | solution.py:36
  116.6 23.3 %collective-permute-start.18 = (f32[2,256,128]{2,1,0:T(8,128)S(1)}, f32[2,256,128]{2,1,0:T(8,128)S(1)}, u32[]{:S(2)}, u32[]{:S(2)}) collective-permute-start(f32[2,256,128]{2,1,0:T(8,128)S(1)} %reverse_add_fusion.near), channel_id=1, source_target_pairs={{0,4},{1,5},{2,6},{3,7},{4,0},{5,1},{6,2},{7,3},{8,12},{9,13},{10,... | collective-permute-start | bytes 786440 | tf_op jit(solution)/shard_map/ppermute | solution.py:36
  121.1 19.4 %collective-permute-start.16 = (f32[2,256,128]{2,1,0:T(8,128)S(1)}, f32[2,256,128]{2,1,0:T(8,128)S(1)}, u32[]{:S(2)}, u32[]{:S(2)}) collective-permute-start(f32[2,256,128]{2,1,0:T(8,128)S(1)} %reverse_add_fusion.near), channel_id=1, source_target_pairs={{0,6},{1,7},{2,4},{3,5},{4,2},{5,3},{6,0},{7,1},{8,14},{9,15},{10,... | collective-permute-start | bytes 786440 | tf_op jit(solution)/shard_map/ppermute | solution.py:36
  128.8 16.3 %collective-permute-start.21 = (f32[2,256,128]{2,1,0:T(8,128)S(1)}, f32[2,256,128]{2,1,0:T(8,128)S(1)}, u32[]{:S(2)}, u32[]{:S(2)}) collective-permute-start(f32[2,256,128]{2,1,0:T(8,128)S(1)} %collective-permute-done.20.near), channel_id=1, source_target_pairs={{0,1},{1,0},{2,3},{3,2},{4,5},{5,4},{6,7},{7,6},{8,9},{9,8},{10,11... | collective-permute-start | bytes 786440 | tf_op jit(solution)/shard_map/ppermute | solution.py:36
  139.9 8.9 %collective-permute-start.19 = (f32[2,256,128]{2,1,0:T(8,128)S(1)}, f32[2,256,128]{2,1,0:T(8,128)S(1)}, u32[]{:S(2)}, u32[]{:S(2)}) collective-permute-start(f32[2,256,128]{2,1,0:T(8,128)S(1)} %collective-permute-done.18.near), channel_id=1, source_target_pairs={{0,1},{1,0},{2,3},{3,2},{4,5},{5,4},{6,7},{7,6},{8,9},{9,8},{10,11... | collective-permute-start | bytes 786440 | tf_op jit(solution)/shard_map/ppermute | solution.py:36
  140.5 12.1 %collective-permute-start.17 = (f32[2,256,128]{2,1,0:T(8,128)S(1)}, f32[2,256,128]{2,1,0:T(8,128)S(1)}, u32[]{:S(2)}, u32[]{:S(2)}) collective-permute-start(f32[2,256,128]{2,1,0:T(8,128)S(1)} %collective-permute-done.16.near), channel_id=1, source_target_pairs={{0,1},{1,0},{2,3},{3,2},{4,5},{5,4},{6,7},{7,6},{8,9},{9,8},{10,11... | collective-permute-start | bytes 786440 | tf_op jit(solution)/shard_map/ppermute | solution.py:36
  153.5 9.2 %collective-permute-start.23 = (f32[512,128]{1,0:T(8,128)S(1)}, f32[512,128]{1,0:T(8,128)S(1)}, u32[]{:S(2)}, u32[]{:S(2)}) collective-permute-start(f32[512,128]{1,0:T(8,128)S(1)} %predict.11), channel_id=1, source_target_pairs={{0,64},{16,80},{32,96},{48,112},{64,0},{80,16},{96,32},{112,48},{1... | collective-permute-start | bytes 786440 | tf_op jit(solution)/shard_map/ppermute | solution.py:36
  155.5 13.5 %collective-permute-start.24 = (f32[512,128]{1,0:T(8,128)S(1)}, f32[512,128]{1,0:T(8,128)S(1)}, u32[]{:S(2)}, u32[]{:S(2)}) collective-permute-start(f32[512,128]{1,0:T(8,128)S(1)} %predict.12), channel_id=1, source_target_pairs={{0,128},{16,144},{32,160},{48,176},{64,192},{80,208},{96,224},{112... | collective-permute-start | bytes 786440 | tf_op jit(solution)/shard_map/ppermute | solution.py:36
  158.9 15.0 %collective-permute-start.25 = (f32[512,128]{1,0:T(8,128)S(1)}, f32[512,128]{1,0:T(8,128)S(1)}, u32[]{:S(2)}, u32[]{:S(2)}) collective-permute-start(f32[512,128]{1,0:T(8,128)S(1)} %predict.13), channel_id=1, source_target_pairs={{0,192},{16,208},{32,224},{48,240},{64,128},{80,144},{96,160},{112... | collective-permute-start | bytes 786440 | tf_op jit(solution)/shard_map/ppermute | solution.py:36
  174.0 4.4 %collective-permute-start.26 = (f32[128,128]{1,0:T(8,128)S(1)}, f32[128,128]{1,0:T(8,128)S(1)}, u32[]{:S(2)}, u32[]{:S(2)}) collective-permute-start(f32[128,128]{1,0:T(8,128)S(1)} %get-tuple-element.56), channel_id=1, source_target_pairs={{0,16},{16,0},{32,48},{48,32},{64,80},{80,64},{96,112},{112,96},{1... | collective-permute-start | bytes 196616 | tf_op jit(solution)/shard_map/ppermute | solution.py:36
  174.1 6.4 %collective-permute-start.27 = (f32[128,128]{1,0:T(8,128)S(1)}, f32[128,128]{1,0:T(8,128)S(1)}, u32[]{:S(2)}, u32[]{:S(2)}) collective-permute-start(f32[128,128]{1,0:T(8,128)S(1)} %get-tuple-element.55), channel_id=1, source_target_pairs={{0,32},{16,48},{32,0},{48,16},{64,96},{80,112},{96,64},{112,80},{1... | collective-permute-start | bytes 196616 | tf_op jit(solution)/shard_map/ppermute | solution.py:36
  176.2 6.5 %collective-permute-start.28 = (f32[128,128]{1,0:T(8,128)S(1)}, f32[128,128]{1,0:T(8,128)S(1)}, u32[]{:S(2)}, u32[]{:S(2)}) collective-permute-start(f32[128,128]{1,0:T(8,128)S(1)} %get-tuple-element.54), channel_id=1, source_target_pairs={{0,48},{16,32},{32,16},{48,0},{64,112},{80,96},{96,80},{112,64},{1... | collective-permute-start | bytes 196616 | tf_op jit(solution)/shard_map/ppermute | solution.py:36
